TPU v7x, 32 devices: a whole 2x2x4 slice. The times are simulated.
32 devices in a mesh: pair: 2 (over x), grow: 4 (over y, core), gcol: 4 (over z).
Axes of the slice: x: 2, y: 2, z: 4, core: 2. Of those that a mesh axis runs over, the one named last changes fastest.
Arguments:
- pair_elements: bfloat16 [1792, 8192], P('pair', ('grow', 'gcol')), may hold values from -0.75 to 0.75
- coulomb_root: float32 [8192], replicated, may hold values from 0.25 to 1
Outputs:
- factored: float32 [8192, 8192], P('grow', ('gcol', 'pair'))
All inputs are finite; a program needn't handle non-finite values.
Results may differ from a plain program's by a relative error of at most 0.0003.
Values may be sent and summed in bfloat16 or wider, within the bound.
A program may use at most 128 MiB of HBM per device.

v0:
```python
import jax
import jax.numpy as jnp
from jax import lax
from jax.sharding import PartitionSpec as P

PANEL = 512
PANELS = 2


def from_root(array, axis, root):
    mine = lax.axis_index(axis) == root
    return lax.psum(jnp.where(mine, array, jnp.zeros_like(array)), axis)


def body(pair_elements, coulomb_root):
    grid_total = coulomb_root.shape[0]
    tile_rows = grid_total // lax.axis_size("grow")
    tile_cols = grid_total // (lax.axis_size("gcol") * lax.axis_size("pair"))
    row_index = lax.axis_index("grow")
    col_index = lax.axis_index("gcol")
    gathered = lax.all_gather(pair_elements, ("grow", "gcol"), axis=1, tiled=True)
    row_block = lax.dynamic_slice_in_dim(gathered, row_index * tile_rows, tile_rows, 1)
    col_block = lax.dynamic_slice_in_dim(gathered, col_index * tile_rows, tile_rows, 1)
    flipped = lax.psum_scatter(
        lax.dot_general(
            col_block, row_block, (((0,), (0,)), ((), ())), preferred_element_type=jnp.float32
        ),
        "pair",
        scatter_dimension=0,
        tiled=True,
    )
    chi_tile = flipped.T
    row_base = row_index * tile_rows
    col_base = lax.axis_index(("gcol", "pair")) * tile_cols
    row_ids = row_base + jnp.arange(tile_rows, dtype=jnp.int32)[:, None]
    col_ids = col_base + jnp.arange(tile_cols, dtype=jnp.int32)[None, :]
    scale_rows = lax.dynamic_slice_in_dim(coulomb_root, row_base, tile_rows, 0)
    scale_cols = lax.dynamic_slice_in_dim(coulomb_root, col_base, tile_cols, 0)
    working = (
        jnp.where(row_ids == col_ids, 1.0, 0.0).astype(jnp.float32)
        + scale_rows[:, None] * chi_tile * scale_cols[None, :]
    )
    packed = jnp.zeros((tile_rows, tile_cols), jnp.float32)
    covered = jnp.zeros((tile_rows, tile_cols), bool)
    owner_width = min(PANEL, tile_cols)
    for step_index in range(PANELS):
        first = step_index * PANEL
        gathered_cols = []
        for owner in range(max(1, PANEL // tile_cols)):
            global_col = first + owner * owner_width
            local_col = global_col % tile_cols
            gathered_cols.append(
                from_root(
                    working[:, local_col : local_col + owner_width],
                    ("gcol", "pair"),
                    global_col // tile_cols,
                )
            )
        panel_cols = jnp.concatenate(gathered_cols, axis=1)
        local_row = first % tile_rows
        diag_block, panel_rows = (
            from_root(panel_cols[local_row : local_row + PANEL], "grow", first // tile_rows),
            from_root(working[local_row : local_row + PANEL], "grow", first // tile_rows),
        )
        factor = jnp.linalg.cholesky(diag_block)
        low_rows = lax.linalg.triangular_solve(
            factor, panel_cols, left_side=False, lower=True, transpose_a=True
        )
        low_cols = lax.linalg.triangular_solve(factor, panel_rows, left_side=True, lower=True)
        working = working - jnp.dot(low_rows, low_cols, precision=lax.Precision.HIGHEST)
        col_pos = col_ids - first
        in_cols = (col_pos >= 0) & (col_pos < PANEL) & (row_ids >= col_ids)
        col_vals = jnp.take(low_rows, jnp.clip(col_pos[0], 0, PANEL - 1), axis=1)
        row_pos = row_ids - first
        in_rows = (row_pos >= 0) & (row_pos < PANEL) & (col_ids > row_ids)
        row_vals = jnp.take(low_cols, jnp.clip(row_pos[:, 0], 0, PANEL - 1), axis=0)
        packed = packed + jnp.where(in_cols, col_vals, 0.0) + jnp.where(in_rows, row_vals, 0.0)
        covered = covered | in_cols | in_rows
    return jnp.where(covered, packed, working)


def solution(mesh):
    return jax.shard_map(
        body,
        mesh=mesh,
        in_specs=(P("pair", ("grow", "gcol")), P()),
        out_specs=P("grow", ("gcol", "pair")),
        check_vma=False,
    )
```

profile of v0, /device:TPU:0, one launch (start us, length us, event | category | flops | bytes accessed | tf_op | source)
XLA Modules:
  0.0 1215.4 jit_solution(15277184497236068876)
XLA Ops:
  7.3 122.0 %all-gather.2.cloned.1.call-done = bf16[896,8192]{1,0:T(8,128)(2,1)} async-done(((bf16[896,512]{1,0:T(8,128)(2,1)}), bf16[896,8192]{1,0:T(8,128)(2,1)}) %all-gather.2.cloned.1.call-update) | async-done | bytes 14680080 | tf_op jit(solution)/shard_map/all_gather | solution.py:21
  129.3 15.1 %fusion.11 = f32[2048,2048]{1,0:T(8,128)} fusion(bf16[896,8192]{1,0:T(8,128)(2,1)} %all-gather.2.cloned.1.call-done, s32[]{:T(128)} %select_n.87, s32[]{:T(128)S(6)} %select_n.88), kind=kOutput, calls=%fused_computation.29 | convolution fusion | flops 7516192768 | bytes 24117764 | tf_op jit(solution)/shard_map/dot_general | solution.py:25
  145.1 186.7 %reduce-scatter.2.cloned.1.call-done = f32[1024,2048]{1,0:T(8,128)} async-done(((f32[2048,2048]{1,0:T(8,128)}), f32[1024,2048]{1,0:T(8,128)}) %reduce-scatter.2.cloned.1.call-update) | async-done | bytes 8388624 | tf_op jit(solution)/shard_map/reduce_scatter | solution.py:24
  331.8 4.3 bitcast_add_fusion
  336.1 3.4 copy-done
  339.5 2.5 slice_select_fusion.1
  342.1 3.2 slice_select_fusion.3
  345.3 153.2 %all-reduce.8.cloned.1.call-done = f32[2048,512]{0,1:T(8,128)} async-done(((f32[2048,512]{0,1:T(8,128)}), f32[2048,512]{0,1:T(8,128)}) %all-reduce.8.cloned.1.call-update) | async-done | bytes 4194320 | tf_op jit(solution)/shard_map/psum | solution.py:12
  498.5 2.3 slice_select_fusion.5
  501.4 67.2 %all-reduce.14.cloned.1.call-done = (f32[512,1024]{0,1:T(8,128)}, f32[512,512]{0,1:T(8,128)}) async-done(((f32[512,1024]{0,1:T(8,128)}, f32[512,512]{0,1:T(8,128)}), (f32[512,1024]{0,1:T(8,128)}, f32[512,512]{0,1:T(8,128)})) %all-reduce.14.cloned.1.call-update) | async-done | bytes 3145744 | tf_op jit(solution)/shard_map/psum | solution.py:12
  568.7 1.6 copy.3
  571.7 11.7 cholesky.286
  583.6 9.8 custom-call.31
  594.1 11.7 cholesky.305
  605.8 10.0 custom-call.32
  616.4 11.7 cholesky.326
  628.2 9.8 custom-call.33
  638.6 11.7 cholesky.343
  655.3 7.7 while.8
  663.0 39.3 %custom-call.34 = f32[4,128,128]{1,2,0:T(8,128)S(1)} custom-call(f32[4,128,128]{2,1,0:T(8,128)S(1)} %get-tuple-element.38), custom_call_target="InvertDiagBlocksLowerTriangular" | custom-call | tf_op jit(solution)/shard_map/triangular_solve/custom-call.3 | solution.py:66
  702.3 1.8 fusion.70
  704.2 2.2 convolution_subtract_fusion.8
  707.1 1.8 convolution_subtract_fusion.6
  709.6 2.8 fusion.53
  712.3 1.5 fusion.106
  717.1 2.9 convolution_subtract_fusion.2
  721.1 3.7 fusion.29
  724.8 2.1 fusion.107
  727.0 17.2 %convolution_subtract_fusion = f32[2048,1024]{0,1:T(8,128)S(1)} fusion(f32[2048,1024]{0,1:T(8,128)S(1)} %bitcast.135, f32[128,1024]{1,0:T(8,128)} %fusion.106, f32[128,1024]{1,0:T(8,128)} %copy-done.9, f32[128,1024]{1,0:T(8,128)} %copy-done.7, f32[128,1024]{1,0:T(8,128)} %copy-done.4, f32[2048,128]{0,1:T(8,128)} %fusion.107, f32[2048,128]{0,1:T(8,128)} %copy-done.5, ...), kind=kOutput, calls=%fused_computation.28 | convolution fusion | flops 12891717632 | bytes 23068672 | tf_op jit(solution)/shard_map/dot_general | solution.py:70
  744.2 3.4 copy-done.1
  747.6 2.3 slice_select_fusion
  749.9 3.2 slice_select_fusion.2
  753.1 153.3 %all-reduce.10.cloned.1.call-done = f32[2048,512]{0,1:T(8,128)} async-done(((f32[2048,512]{0,1:T(8,128)}), f32[2048,512]{0,1:T(8,128)}) %all-reduce.10.cloned.1.call-update) | async-done | bytes 4194320 | tf_op jit(solution)/shard_map/psum | solution.py:12
  906.4 2.3 slice_select_fusion.4
  908.8 1.7 pad_maximum_fusion.2
  910.5 9.8 gather_fusion.1
  920.3 9.5 copy.4
  929.8 3.5 pad_maximum_fusion
  933.3 11.6 gather_fusion
  944.9 31.7 %all-reduce.12.cloned.1.call-done = (f32[512,1024]{0,1:T(8,128)}, f32[512,512]{0,1:T(8,128)}) async-done(((f32[512,1024]{0,1:T(8,128)}, f32[512,512]{0,1:T(8,128)}), (f32[512,1024]{0,1:T(8,128)}, f32[512,512]{0,1:T(8,128)})) %all-reduce.12.cloned.1.call-update) | async-done | bytes 3145744 | tf_op jit(solution)/shard_map/psum | solution.py:12
  976.6 1.6 copy.6
  979.6 11.7 cholesky.358
  991.5 9.8 custom-call.36
  1002.0 11.7 cholesky.377
  1013.7 10.0 custom-call.37
  1024.4 11.7 cholesky.398
  1036.1 9.8 custom-call.38
  1046.5 11.7 cholesky.415
  1064.1 8.2 while.9
  1072.3 39.3 %custom-call.39 = f32[4,128,128]{1,2,0:T(8,128)S(1)} custom-call(f32[4,128,128]{2,1,0:T(8,128)S(1)} %get-tuple-element.40), custom_call_target="InvertDiagBlocksLowerTriangular" | custom-call | tf_op jit(solution)/shard_map/triangular_solve/custom-call.3 | solution.py:66
  1111.7 1.8 fusion.68
  1113.5 2.0 convolution_subtract_fusion.7
  1116.2 1.8 convolution_subtract_fusion.5
  1118.7 2.7 fusion.50
  1122.9 9.8 gather_fusion.3
  1132.7 9.6 copy.7
  1142.3 2.4 fusion.56
  1144.7 2.3 convolution_subtract_fusion.3
  1148.1 2.2 convolution_subtract_fusion.1
  1151.5 3.3 fusion.26
  1155.9 2.4 pad_maximum_fusion.1
  1158.4 11.2 gather_fusion.2
  1169.6 29.6 %fusion.8 = f32[2048,1024]{0,1:T(8,128)} fusion(f32[2048,1024]{0,1:T(8,128)} %copy.7, f32[1024,2048]{1,0:T(8,128)} %gather_fusion.2, f32[2048,1024]{0,1:T(8,128)} %copy.4, f32[1024,2048]{1,0:T(8,128)} %gather_fusion, f32[2048,1024]{0,1:T(8,128)} %copy-done.1, s32[2048]{0:T(1024)S(1)} %iota_add_fusion, pred[1024]{0:T(1024)(128)(4,1)S(1)} %get-tuple-element.98, ...), kind=kOutput, calls=%fused_computation.20 | convolution fusion | flops 12935757824 | bytes 56647680 | tf_op jit(solution)/shard_map/dot_general | solution.py:70
  1199.2 9.2 copy.9
  (146 shorter events, 42.0 us)
Async XLA Ops:
  6.5 122.7 %all-gather.2.cloned.1.call-start = ((), (), s32[]{:S(2)}) async-start(), calls=%async_computation.1 | async-start | bytes 15597568 | tf_op jit(solution)/shard_map/all_gather | solution.py:21
  7.3 324.5 %reduce-scatter.2.cloned.1.call-start = ((), (), s32[]{:S(2)}) async-start(), calls=%async_computation.2 | async-start | bytes 25165824 | tf_op jit(solution)/shard_map/reduce_scatter | solution.py:24
  144.3 0.8 copy-start.19
  144.3 187.5 %dynamic-slice-start = ((f32[8192]{0:T(1024)}, s32[]{:T(128)}), f32[2048]{0:T(1024)S(1)}, s32[]{:S(2)}) async-start(f32[8192]{0:T(1024)} %param.12, s32[]{:T(128)} %select_n.87), calls=%async_computation.9 | async-start | bytes 16896 | tf_op jit(solution)/shard_map/dynamic_slice | solution.py:37
  144.4 354.1 %all-reduce.8.cloned.1.call-start = ((), (), s32[]{:S(2)}) async-start(), calls=%async_computation.3 | async-start | bytes 8388608 | tf_op jit(solution)/shard_map/psum | solution.py:12
  336.1 3.4 copy-start
  342.0 226.6 %all-reduce.14.cloned.1.call-start = ((), (), s32[]{:S(2)}) async-start(), calls=%async_computation.6 | async-start | bytes 6291456 | tf_op jit(solution)/shard_map/psum | solution.py:12
  500.8 405.6 %all-reduce.10.cloned.1.call-start = ((), (), s32[]{:S(2)}) async-start(), calls=%async_computation.4 | async-start | bytes 8388608 | tf_op jit(solution)/shard_map/psum | solution.py:12
  663.0 51.9 %copy-start.14 = (f32[512,512]{1,0:T(8,128)}, f32[512,512]{1,0:T(8,128)S(1)}, u32[]{:S(2)}) copy-start(f32[512,512]{1,0:T(8,128)S(1)} %get-tuple-element.218) | copy-start | bytes 3145732
  702.3 4.8 copy-start.17
  704.2 8.2 copy-start.4
  706.4 7.4 copy-start.11
  707.1 7.8 copy-start.7
  709.6 6.4 copy-start.9
  716.0 11.0 slice-start
  717.1 9.9 copy-start.2
  720.0 6.9 slice-start.1
  721.1 3.7 copy-start.5
  744.2 3.4 copy-start.1
  749.9 226.7 %all-reduce.12.cloned.1.call-start = ((), (), s32[]{:S(2)}) async-start(), calls=%async_computation.5 | async-start | bytes 6291456 | tf_op jit(solution)/shard_map/psum | solution.py:12
  920.3 9.5 copy-start.3
  920.3 9.5 copy-start.6
  1072.3 49.1 %copy-start.13 = (f32[512,512]{1,0:T(8,128)}, f32[512,512]{1,0:T(8,128)S(1)}, u32[]{:S(2)}) copy-start(f32[512,512]{1,0:T(8,128)S(1)} %get-tuple-element.217) | copy-start | bytes 3145732
  1111.7 4.5 copy-start.16
  1118.7 3.4 copy-start.12
  1122.1 0.8 copy-start.18
  1142.3 5.9 copy-start.10
  1151.5 6.9 copy-start.8
  1155.9 2.5 copy-start.15
Sparse Core Ops, SparseCore 0:
  9.4 119.7 all-gather.1
  144.5 187.2 reduce-scatter.1
  342.1 156.2 all-reduce.7
  501.0 67.6 all-reduce.13
  750.0 156.3 all-reduce.9
  908.9 67.6 all-reduce.11
where the time goes:
time: 1220 us
  waiting for transfers between devices  715 us (59%)
  other arithmetic  268 us (22%)
  matrix products  114 us (9%)
  local copies, waits for them, and re-layouts  98 us (8%)
  between operations  20 us (2%)
    psum x4, waiting for transfers between devices, from_root(): return lax.psum(jnp.where(mine, array, jnp.zeros_like(array)), axis)  405 us
    reduce_scatter x1, waiting for transfers between devices, body(): lax.psum_scatter(lax.dot_general(col_block, row_block, (((0,), (0,)), (()...  187 us
    another operation x29, other arithmetic, body(): factor = jnp.linalg.cholesky(diag_block)  158 us
    all_gather x1, waiting for transfers between devices, body(): lax.all_gather(pair_elements, ('grow', 'gcol'), axis=1, tiled=True)  122 us
    another operation x7, other arithmetic, body(): lax.linalg.triangular_solve(factor, panel_cols, left_side=False, lower=Tr...  85 us
    dot_general x2, matrix products, body(): jnp.dot(low_rows, low_cols, precision=lax.Precision.HIGHEST)  46.8 us
    gather x4, local copies, waits for them, and re-layouts, body(): row_vals = jnp.take(low_cols, jnp.clip(row_pos[:, 0], 0, PANEL - 1), axis=0)  38.7 us
    another operation x14, matrix products, body(): lax.linalg.triangular_solve(factor, panel_cols, left_side=False, lower=Tr...  26.6 us
  transfers between devices with their start and end apart: 6, of which 6 were waited for; matrix products, arithmetic and copies ran while one was open for 3% of the time, Pallas kernels for 0%

commit v1 on v0

--- a/solution.py
+++ b/solution.py
@@ -5,6 +5,27 @@
 
 PANEL = 512
 PANELS = 2
+
+
+def ring_gather(array, axis, dim):
+    devices, place, rows = (lax.axis_size(axis), lax.axis_index(axis), array.shape[dim])
+    right = [(i, (i + 1) % devices) for i in range(devices)]
+    left = [(i, (i - 1) % devices) for i in range(devices)]
+    filled = jnp.zeros((*array.shape[:dim], devices * rows, *array.shape[dim + 1 :]), array.dtype)
+    filled = lax.dynamic_update_slice_in_dim(filled, array, place * rows, axis=dim)
+    from_left = from_right = array
+    middle = devices // 2
+    for hop in range(1, middle + 1):
+        from_left = lax.ppermute(from_left, axis, right)
+        filled = lax.dynamic_update_slice_in_dim(
+            filled, from_left, (place - hop) % devices * rows, axis=dim
+        )
+        if hop < devices - middle:
+            from_right = lax.ppermute(from_right, axis, left)
+            filled = lax.dynamic_update_slice_in_dim(
+                filled, from_right, (place + hop) % devices * rows, axis=dim
+            )
+    return filled
 
 
 def from_root(array, axis, root):
@@ -18,7 +39,7 @@
     tile_cols = grid_total // (lax.axis_size("gcol") * lax.axis_size("pair"))
     row_index = lax.axis_index("grow")
     col_index = lax.axis_index("gcol")
-    gathered = lax.all_gather(pair_elements, ("grow", "gcol"), axis=1, tiled=True)
+    gathered = ring_gather(pair_elements, ("grow", "gcol"), 1)
     row_block = lax.dynamic_slice_in_dim(gathered, row_index * tile_rows, tile_rows, 1)
     col_block = lax.dynamic_slice_in_dim(gathered, col_index * tile_rows, tile_rows, 1)
     flipped = lax.psum_scatter(

time: 1220 us -> 1410 us (1.16)
  waiting for transfers between devices: 715 us -> 841 us
  local copies, waits for them, and re-layouts: 98 us -> 129 us
  starting transfers between devices: 0.73 us -> 25.2 us
    ppermute x0 -> x15, waiting for transfers between devices: none -> 244 us  [the longest x7 139 us: ring_gather(): from_right = lax.ppermute(from_right, axis, left)]
    all_gather x1 -> x0, waiting for transfers between devices: 122 us -> none  [body(): lax.all_gather(pair_elements, ('grow', 'gcol'), axis=1, tiled=True)]
    ppermute x0 -> x15, starting transfers between devices: none -> 24.9 us  [the longest x8 18.1 us: ring_gather(): from_left = lax.ppermute(from_left, axis, right)]
    dynamic_update_slice x0 -> x16, local copies, waits for them, and re-layouts: none -> 22.4 us  [the longest x7 10.8 us: ring_gather(): lax.dynamic_update_slice_in_dim(filled, from_right, (place + hop) % devic...]
  transfers between devices with their start and end apart: 6 -> 20, of which waited for: 6 -> 20; matrix products, arithmetic and copies ran while one was open for 3% -> 5% of each run, Pallas kernels for 0% -> 0%
where the time goes in v1:
time: 1410 us; the launch traced here: 1400 us
  waiting for transfers between devices  841 us (60%)
  other arithmetic  269 us (19%)
  local copies, waits for them, and re-layouts  129 us (9%)
  matrix products  114 us (8%)
  starting transfers between devices  25.2 us (2%)
  between operations  19.3 us (1%)
    psum x4, waiting for transfers between devices, from_root(): return lax.psum(jnp.where(mine, array, jnp.zeros_like(array)), axis)  406 us
    reduce_scatter x1, waiting for transfers between devices, body(): lax.psum_scatter(lax.dot_general(col_block, row_block, (((0,), (0,)), (()...  190 us
    another operation x29, other arithmetic, body(): factor = jnp.linalg.cholesky(diag_block)  158 us
    ppermute x7, waiting for transfers between devices, ring_gather(): from_right = lax.ppermute(from_right, axis, left)  139 us
    ppermute x8, waiting for transfers between devices, ring_gather(): from_left = lax.ppermute(from_left, axis, right)  105 us
    another operation x7, other arithmetic, body(): lax.linalg.triangular_solve(factor, panel_cols, left_side=False, lower=Tr...  85.4 us
    dot_general x2, matrix products, body(): jnp.dot(low_rows, low_cols, precision=lax.Precision.HIGHEST)  46.9 us
    gather x4, local copies, waits for them, and re-layouts, body(): row_vals = jnp.take(low_cols, jnp.clip(row_pos[:, 0], 0, PANEL - 1), axis=0)  38.4 us
  transfers between devices with their start and end apart: 20, of which 20 were waited for; matrix products, arithmetic and copies ran while one was open for 5% of the time, Pallas kernels for 0%

profile of v1, /device:TPU:0, one launch (start us, length us, event | category | flops | bytes accessed | tf_op | source)
XLA Modules:
  0.0 1396.7 jit_solution(17436879968313937015)
XLA Ops:
  6.5 3.0 collective-permute-start
  12.0 20.4 %collective-permute-done = bf16[896,512]{1,0:T(8,128)(2,1)S(1)} collective-permute-done((bf16[896,512]{1,0:T(8,128)(2,1)}, bf16[896,512]{1,0:T(8,128)(2,1)S(1)}, u32[]{:S(2)}, u32[]{:S(2)}) %collective-permute-start) | collective-permute-done | bytes 917536 | tf_op jit(solution)/shard_map/ppermute | solution.py:19
  33.0 18.2 %collective-permute-done.1 = bf16[896,512]{1,0:T(8,128)(2,1)S(1)} collective-permute-done((bf16[896,512]{1,0:T(8,128)(2,1)}, bf16[896,512]{1,0:T(8,128)(2,1)S(1)}, u32[]{:S(2)}, u32[]{:S(2)}) %collective-permute-start.1) | collective-permute-done | bytes 917536 | tf_op jit(solution)/shard_map/ppermute | solution.py:24
  51.2 3.6 collective-permute-start.3
  54.8 15.4 %collective-permute-done.2 = bf16[896,512]{1,0:T(8,128)(2,1)S(1)} collective-permute-done((bf16[896,512]{1,0:T(8,128)(2,1)S(1)}, bf16[896,512]{1,0:T(8,128)(2,1)S(1)}, u32[]{:S(2)}, u32[]{:S(2)}) %collective-permute-start.2) | collective-permute-done | bytes 917536 | tf_op jit(solution)/shard_map/ppermute | solution.py:19
  72.4 21.1 %collective-permute-done.3 = bf16[896,512]{1,0:T(8,128)(2,1)S(1)} collective-permute-done((bf16[896,512]{1,0:T(8,128)(2,1)S(1)}, bf16[896,512]{1,0:T(8,128)(2,1)S(1)}, u32[]{:S(2)}, u32[]{:S(2)}) %collective-permute-start.3) | collective-permute-done | bytes 917536 | tf_op jit(solution)/shard_map/ppermute | solution.py:24
  94.2 15.0 %collective-permute-done.4 = bf16[896,512]{1,0:T(8,128)(2,1)S(1)} collective-permute-done((bf16[896,512]{1,0:T(8,128)(2,1)S(1)}, bf16[896,512]{1,0:T(8,128)(2,1)S(1)}, u32[]{:S(2)}, u32[]{:S(2)}) %collective-permute-start.4) | collective-permute-done | bytes 917536 | tf_op jit(solution)/shard_map/ppermute | solution.py:19
  111.8 22.1 %collective-permute-done.5 = bf16[896,512]{1,0:T(8,128)(2,1)S(1)} collective-permute-done((bf16[896,512]{1,0:T(8,128)(2,1)S(1)}, bf16[896,512]{1,0:T(8,128)(2,1)S(1)}, u32[]{:S(2)}, u32[]{:S(2)}) %collective-permute-start.5) | collective-permute-done | bytes 917536 | tf_op jit(solution)/shard_map/ppermute | solution.py:24
  133.9 14.7 %collective-permute-done.6 = bf16[896,512]{1,0:T(8,128)(2,1)S(1)} collective-permute-done((bf16[896,512]{1,0:T(8,128)(2,1)S(1)}, bf16[896,512]{1,0:T(8,128)(2,1)S(1)}, u32[]{:S(2)}, u32[]{:S(2)}) %collective-permute-start.6) | collective-permute-done | bytes 917536 | tf_op jit(solution)/shard_map/ppermute | solution.py:19
  152.1 22.2 %collective-permute-done.7 = bf16[896,512]{1,0:T(8,128)(2,1)} collective-permute-done((bf16[896,512]{1,0:T(8,128)(2,1)S(1)}, bf16[896,512]{1,0:T(8,128)(2,1)}, u32[]{:S(2)}, u32[]{:S(2)}) %collective-permute-start.7) | collective-permute-done | bytes 917536 | tf_op jit(solution)/shard_map/ppermute | solution.py:24
  174.3 13.7 collective-permute-done.8
  188.0 2.6 collective-permute-start.10
  190.6 23.8 %collective-permute-done.9 = bf16[896,512]{1,0:T(8,128)(2,1)} collective-permute-done((bf16[896,512]{1,0:T(8,128)(2,1)}, bf16[896,512]{1,0:T(8,128)(2,1)}, u32[]{:S(2)}, u32[]{:S(2)}) %collective-permute-start.9) | collective-permute-done | bytes 917536 | tf_op jit(solution)/shard_map/ppermute | solution.py:24
  214.4 7.0 broadcast_in_dim.41
  222.5 5.0 collective-permute-done.10
  236.0 18.4 %collective-permute-done.11 = bf16[896,512]{1,0:T(8,128)(2,1)} collective-permute-done((bf16[896,512]{1,0:T(8,128)(2,1)}, bf16[896,512]{1,0:T(8,128)(2,1)}, u32[]{:S(2)}, u32[]{:S(2)}) %collective-permute-start.11) | collective-permute-done | bytes 917536 | tf_op jit(solution)/shard_map/ppermute | solution.py:24
  255.5 11.4 collective-permute-done.12
  281.5 12.8 collective-permute-done.13
  295.3 9.6 collective-permute-done.14
  306.0 14.9 %fusion.11 = f32[2048,2048]{1,0:T(8,128)} fusion(bf16[896,8192]{1,0:T(8,128)(2,1)} %constant_dynamic-update-slice_fusion.2, s32[]{:T(128)} %select_n.198, s32[]{:T(128)S(6)} %select_n.230), kind=kOutput, calls=%fused_computation.29 | convolution fusion | flops 7516192768 | bytes 24117764 | tf_op jit(solution)/shard_map/dot_general | solution.py:46
  321.7 190.4 %reduce-scatter.2.cloned.1.call-done = f32[1024,2048]{1,0:T(8,128)} async-done(((f32[2048,2048]{1,0:T(8,128)}), f32[1024,2048]{1,0:T(8,128)}) %reduce-scatter.2.cloned.1.call-update) | async-done | bytes 8388624 | tf_op jit(solution)/shard_map/reduce_scatter | solution.py:45
  512.1 4.3 bitcast_add_fusion
  516.4 3.4 copy-done
  519.8 2.6 slice_select_fusion.1
  522.4 3.2 slice_select_fusion.3
  525.6 153.2 %all-reduce.8.cloned.1.call-done = f32[2048,512]{0,1:T(8,128)} async-done(((f32[2048,512]{0,1:T(8,128)}), f32[2048,512]{0,1:T(8,128)}) %all-reduce.8.cloned.1.call-update) | async-done | bytes 4194320 | tf_op jit(solution)/shard_map/psum | solution.py:33
  681.4 67.7 %all-reduce.14.cloned.1.call-done = (f32[512,1024]{0,1:T(8,128)}, f32[512,512]{0,1:T(8,128)}) async-done(((f32[512,1024]{0,1:T(8,128)}, f32[512,512]{0,1:T(8,128)}), (f32[512,1024]{0,1:T(8,128)}, f32[512,512]{0,1:T(8,128)})) %all-reduce.14.cloned.1.call-update) | async-done | bytes 3145744 | tf_op jit(solution)/shard_map/psum | solution.py:33
  752.1 11.7 cholesky.286
  764.0 9.8 custom-call.31
  774.5 11.7 cholesky.305
  786.2 10.2 custom-call.32
  797.1 11.7 cholesky.326
  808.9 9.8 custom-call.33
  819.3 11.7 cholesky.343
  835.9 8.0 while.8
  843.9 39.3 %custom-call.34 = f32[4,128,128]{1,2,0:T(8,128)S(1)} custom-call(f32[4,128,128]{2,1,0:T(8,128)S(1)} %get-tuple-element.38), custom_call_target="InvertDiagBlocksLowerTriangular" | custom-call | tf_op jit(solution)/shard_map/triangular_solve/custom-call.3 | solution.py:87
  890.5 2.8 fusion.53
  898.0 3.2 convolution_subtract_fusion.2
  902.2 3.7 fusion.29
  908.1 17.2 %convolution_subtract_fusion = f32[2048,1024]{0,1:T(8,128)S(1)} fusion(f32[2048,1024]{0,1:T(8,128)S(1)} %bitcast.135, f32[128,1024]{1,0:T(8,128)} %fusion.106, f32[128,1024]{1,0:T(8,128)} %copy-done.9, f32[128,1024]{1,0:T(8,128)} %copy-done.7, f32[128,1024]{1,0:T(8,128)} %copy-done.4, f32[2048,128]{0,1:T(8,128)} %fusion.107, f32[2048,128]{0,1:T(8,128)} %copy-done.5, ...), kind=kOutput, calls=%fused_computation.28 | convolution fusion | flops 12891717632 | bytes 23068672 | tf_op jit(solution)/shard_map/dot_general | solution.py:91
  925.3 3.4 copy-done.1
  931.1 3.2 slice_select_fusion.2
  934.3 153.3 %all-reduce.10.cloned.1.call-done = f32[2048,512]{0,1:T(8,128)} async-done(((f32[2048,512]{0,1:T(8,128)}), f32[2048,512]{0,1:T(8,128)}) %all-reduce.10.cloned.1.call-update) | async-done | bytes 4194320 | tf_op jit(solution)/shard_map/psum | solution.py:33
  1091.6 9.8 gather_fusion.1
  1101.5 9.4 copy.4
  1110.9 3.5 pad_maximum_fusion
  1114.4 11.3 gather_fusion
  1125.7 32.0 %all-reduce.12.cloned.1.call-done = (f32[512,1024]{0,1:T(8,128)}, f32[512,512]{0,1:T(8,128)}) async-done(((f32[512,1024]{0,1:T(8,128)}, f32[512,512]{0,1:T(8,128)}), (f32[512,1024]{0,1:T(8,128)}, f32[512,512]{0,1:T(8,128)})) %all-reduce.12.cloned.1.call-update) | async-done | bytes 3145744 | tf_op jit(solution)/shard_map/psum | solution.py:33
  1160.7 11.7 cholesky.358
  1172.6 9.8 custom-call.36
  1183.1 11.7 cholesky.377
  1194.9 10.0 custom-call.37
  1205.5 11.7 cholesky.398
  1217.3 9.8 custom-call.38
  1227.7 11.7 cholesky.415
  1245.3 8.7 while.9
  1254.0 39.3 %custom-call.39 = f32[4,128,128]{1,2,0:T(8,128)S(1)} custom-call(f32[4,128,128]{2,1,0:T(8,128)S(1)} %get-tuple-element.40), custom_call_target="InvertDiagBlocksLowerTriangular" | custom-call | tf_op jit(solution)/shard_map/triangular_solve/custom-call.3 | solution.py:87
  1300.4 2.7 fusion.50
  1304.6 9.9 gather_fusion.3
  1314.4 9.3 copy.7
  1332.9 3.3 fusion.26
  1339.8 11.2 gather_fusion.2
  1351.1 29.7 %fusion.8 = f32[2048,1024]{0,1:T(8,128)} fusion(f32[2048,1024]{0,1:T(8,128)} %copy.7, f32[1024,2048]{1,0:T(8,128)} %gather_fusion.2, f32[2048,1024]{0,1:T(8,128)} %copy.4, f32[1024,2048]{1,0:T(8,128)} %gather_fusion, f32[2048,1024]{0,1:T(8,128)} %copy-done.1, s32[2048]{0:T(1024)S(1)} %iota_add_fusion, pred[1024]{0:T(1024)(128)(4,1)S(1)} %get-tuple-element.98, ...), kind=kOutput, calls=%fused_computation.20 | convolution fusion | flops 12935757824 | bytes 56647680 | tf_op jit(solution)/shard_map/dot_general | solution.py:91
  1380.7 9.2 copy.9
  (212 shorter events, 117.4 us)
Async XLA Ops:
  6.5 505.5 %reduce-scatter.2.cloned.1.call-start = ((), (), s32[]{:S(2)}) async-start(), calls=%async_computation.1 | async-start | bytes 25165824 | tf_op jit(solution)/shard_map/reduce_scatter | solution.py:45
  6.5 25.9 %collective-permute-start = (bf16[896,512]{1,0:T(8,128)(2,1)}, bf16[896,512]{1,0:T(8,128)(2,1)S(1)}, u32[]{:S(2)}, u32[]{:S(2)}) collective-permute-start(bf16[896,512]{1,0:T(8,128)(2,1)} %param.11), channel_id=1, source_target_pairs={{0,1},{1,2},{2,3},{3,4},{4,5},{5,6},{6,7},{7,8},{8,9},{9,10},{10,1... | collective-permute-start | bytes 2752520 | tf_op jit(solution)/shard_map/ppermute | solution.py:19
  9.6 41.7 %collective-permute-start.1 = (bf16[896,512]{1,0:T(8,128)(2,1)}, bf16[896,512]{1,0:T(8,128)(2,1)S(1)}, u32[]{:S(2)}, u32[]{:S(2)}) collective-permute-start(bf16[896,512]{1,0:T(8,128)(2,1)} %param.11), channel_id=1, source_target_pairs={{0,15},{1,0},{2,1},{3,2},{4,3},{5,4},{6,5},{7,6},{8,7},{9,8},{10,9... | collective-permute-start | bytes 2752520 | tf_op jit(solution)/shard_map/ppermute | solution.py:24
  32.4 37.9 %collective-permute-start.2 = (bf16[896,512]{1,0:T(8,128)(2,1)S(1)}, bf16[896,512]{1,0:T(8,128)(2,1)S(1)}, u32[]{:S(2)}, u32[]{:S(2)}) collective-permute-start(bf16[896,512]{1,0:T(8,128)(2,1)S(1)} %collective-permute-done), channel_id=1, source_target_pairs={{0,1},{1,2},{2,3},{3,4},{4,5},{5,6},{6,7},{7,8},{8,9},{9,10},{10,1... | collective-permute-start | bytes 2752520 | tf_op jit(solution)/shard_map/ppermute | solution.py:19
  51.2 42.2 %collective-permute-start.3 = (bf16[896,512]{1,0:T(8,128)(2,1)S(1)}, bf16[896,512]{1,0:T(8,128)(2,1)S(1)}, u32[]{:S(2)}, u32[]{:S(2)}) collective-permute-start(bf16[896,512]{1,0:T(8,128)(2,1)S(1)} %collective-permute-done.1), channel_id=1, source_target_pairs={{0,15},{1,0},{2,1},{3,2},{4,3},{5,4},{6,5},{7,6},{8,7},{9,8},{10,9... | collective-permute-start | bytes 2752520 | tf_op jit(solution)/shard_map/ppermute | solution.py:24
  70.3 23.2 %copy-start.20 = (bf16[896,512]{1,0:T(8,128)(2,1)}, bf16[896,512]{1,0:T(8,128)(2,1)S(1)}, u32[]{:S(2)}) copy-start(bf16[896,512]{1,0:T(8,128)(2,1)S(1)} %collective-permute-done.2) | copy-start | bytes 2752516
  70.3 39.0 %collective-permute-start.4 = (bf16[896,512]{1,0:T(8,128)(2,1)S(1)}, bf16[896,512]{1,0:T(8,128)(2,1)S(1)}, u32[]{:S(2)}, u32[]{:S(2)}) collective-permute-start(bf16[896,512]{1,0:T(8,128)(2,1)S(1)} %collective-permute-done.2), channel_id=1, source_target_pairs={{0,1},{1,2},{2,3},{3,4},{4,5},{5,6},{6,7},{7,8},{8,9},{9,10},{10,1... | collective-permute-start | bytes 2752520 | tf_op jit(solution)/shard_map/ppermute | solution.py:19
  93.5 15.8 %copy-start.22 = (bf16[896,512]{1,0:T(8,128)(2,1)}, bf16[896,512]{1,0:T(8,128)(2,1)S(1)}, u32[]{:S(2)}) copy-start(bf16[896,512]{1,0:T(8,128)(2,1)S(1)} %collective-permute-done.3) | copy-start | bytes 2752516
  93.5 40.4 %collective-permute-start.5 = (bf16[896,512]{1,0:T(8,128)(2,1)S(1)}, bf16[896,512]{1,0:T(8,128)(2,1)S(1)}, u32[]{:S(2)}, u32[]{:S(2)}) collective-permute-start(bf16[896,512]{1,0:T(8,128)(2,1)S(1)} %collective-permute-done.3), channel_id=1, source_target_pairs={{0,15},{1,0},{2,1},{3,2},{4,3},{5,4},{6,5},{7,6},{8,7},{9,8},{10,9... | collective-permute-start | bytes 2752520 | tf_op jit(solution)/shard_map/ppermute | solution.py:24
  109.3 78.7 %copy-start.26 = (bf16[896,512]{1,0:T(8,128)(2,1)}, bf16[896,512]{1,0:T(8,128)(2,1)S(1)}, u32[]{:S(2)}) copy-start(bf16[896,512]{1,0:T(8,128)(2,1)S(1)} %collective-permute-done.4) | copy-start | bytes 2752516
  109.3 39.4 %collective-permute-start.6 = (bf16[896,512]{1,0:T(8,128)(2,1)S(1)}, bf16[896,512]{1,0:T(8,128)(2,1)S(1)}, u32[]{:S(2)}, u32[]{:S(2)}) collective-permute-start(bf16[896,512]{1,0:T(8,128)(2,1)S(1)} %collective-permute-done.4), channel_id=1, source_target_pairs={{0,1},{1,2},{2,3},{3,4},{4,5},{5,6},{6,7},{7,8},{8,9},{9,10},{10,1... | collective-permute-start | bytes 2752520 | tf_op jit(solution)/shard_map/ppermute | solution.py:19
  133.9 56.7 %copy-start.28 = (bf16[896,512]{1,0:T(8,128)(2,1)}, bf16[896,512]{1,0:T(8,128)(2,1)S(1)}, u32[]{:S(2)}) copy-start(bf16[896,512]{1,0:T(8,128)(2,1)S(1)} %collective-permute-done.5) | copy-start | bytes 2752516
  133.9 40.4 %collective-permute-start.7 = (bf16[896,512]{1,0:T(8,128)(2,1)S(1)}, bf16[896,512]{1,0:T(8,128)(2,1)}, u32[]{:S(2)}, u32[]{:S(2)}) collective-permute-start(bf16[896,512]{1,0:T(8,128)(2,1)S(1)} %collective-permute-done.5), channel_id=1, source_target_pairs={{0,15},{1,0},{2,1},{3,2},{4,3},{5,4},{6,5},{7,6},{8,7},{9,8},{10,9... | collective-permute-start | bytes 2752520 | tf_op jit(solution)/shard_map/ppermute | solution.py:24
  148.6 1.0 copy-start.24
  149.6 38.4 %collective-permute-start.8 = (bf16[896,512]{1,0:T(8,128)(2,1)S(1)}, bf16[896,512]{1,0:T(8,128)(2,1)}, u32[]{:S(2)}, u32[]{:S(2)}) collective-permute-start(bf16[896,512]{1,0:T(8,128)(2,1)S(1)} %collective-permute-done.6), channel_id=1, source_target_pairs={{0,1},{1,2},{2,3},{3,4},{4,5},{5,6},{6,7},{7,8},{8,9},{9,10},{10,1... | collective-permute-start | bytes 2752520 | tf_op jit(solution)/shard_map/ppermute | solution.py:19
  174.3 40.1 %collective-permute-start.9 = (bf16[896,512]{1,0:T(8,128)(2,1)}, bf16[896,512]{1,0:T(8,128)(2,1)}, u32[]{:S(2)}, u32[]{:S(2)}) collective-permute-start(bf16[896,512]{1,0:T(8,128)(2,1)} %collective-permute-done.7), channel_id=1, source_target_pairs={{0,15},{1,0},{2,1},{3,2},{4,3},{5,4},{6,5},{7,6},{8,7},{9,8},{10,9... | collective-permute-start | bytes 2752520 | tf_op jit(solution)/shard_map/ppermute | solution.py:24
  188.0 39.5 %collective-permute-start.10 = (bf16[896,512]{1,0:T(8,128)(2,1)}, bf16[896,512]{1,0:T(8,128)(2,1)}, u32[]{:S(2)}, u32[]{:S(2)}) collective-permute-start(bf16[896,512]{1,0:T(8,128)(2,1)} %collective-permute-done.8), channel_id=1, source_target_pairs={{0,1},{1,2},{2,3},{3,4},{4,5},{5,6},{6,7},{7,8},{8,9},{9,10},{10,1... | collective-permute-start | bytes 2752520 | tf_op jit(solution)/shard_map/ppermute | solution.py:19
  190.6 30.9 %copy-start.19 = (bf16[896,512]{1,0:T(8,128)(2,1)S(1)}, bf16[896,512]{1,0:T(8,128)(2,1)}, u32[]{:S(2)}) copy-start(bf16[896,512]{1,0:T(8,128)(2,1)} %param.11) | copy-start | bytes 2752516
  214.4 40.0 %collective-permute-start.11 = (bf16[896,512]{1,0:T(8,128)(2,1)}, bf16[896,512]{1,0:T(8,128)(2,1)}, u32[]{:S(2)}, u32[]{:S(2)}) collective-permute-start(bf16[896,512]{1,0:T(8,128)(2,1)} %collective-permute-done.9), channel_id=1, source_target_pairs={{0,15},{1,0},{2,1},{3,2},{4,3},{5,4},{6,5},{7,6},{8,7},{9,8},{10,9... | collective-permute-start | bytes 2752520 | tf_op jit(solution)/shard_map/ppermute | solution.py:24
  221.5 10.5 copy-start.21
  221.5 11.5 copy-start.23
  221.5 12.6 copy-start.27
  222.5 12.5 copy-start.29
  227.5 39.4 %collective-permute-start.12 = (bf16[896,512]{1,0:T(8,128)(2,1)}, bf16[896,512]{1,0:T(8,128)(2,1)S(1)}, u32[]{:S(2)}, u32[]{:S(2)}) collective-permute-start(bf16[896,512]{1,0:T(8,128)(2,1)} %collective-permute-done.10), channel_id=1, source_target_pairs={{0,1},{1,2},{2,3},{3,4},{4,5},{5,6},{6,7},{7,8},{8,9},{9,10},{10,1... | collective-permute-start | bytes 2752520 | tf_op jit(solution)/shard_map/ppermute | solution.py:19
  231.0 23.5 %copy-start.25 = (bf16[896,512]{1,0:T(8,128)(2,1)S(1)}, bf16[896,512]{1,0:T(8,128)(2,1)}, u32[]{:S(2)}) copy-start(bf16[896,512]{1,0:T(8,128)(2,1)} %copy-done.24) | copy-start | bytes 2752516
  254.5 39.8 %collective-permute-start.13 = (bf16[896,512]{1,0:T(8,128)(2,1)}, bf16[896,512]{1,0:T(8,128)(2,1)S(1)}, u32[]{:S(2)}, u32[]{:S(2)}) collective-permute-start(bf16[896,512]{1,0:T(8,128)(2,1)} %collective-permute-done.11), channel_id=1, source_target_pairs={{0,15},{1,0},{2,1},{3,2},{4,3},{5,4},{6,5},{7,6},{8,7},{9,8},{10,9... | collective-permute-start | bytes 2752520 | tf_op jit(solution)/shard_map/ppermute | solution.py:24
  266.8 38.1 %collective-permute-start.14 = (bf16[896,512]{1,0:T(8,128)(2,1)S(1)}, bf16[896,512]{1,0:T(8,128)(2,1)S(1)}, u32[]{:S(2)}, u32[]{:S(2)}) collective-permute-start(bf16[896,512]{1,0:T(8,128)(2,1)S(1)} %collective-permute-done.12), channel_id=1, source_target_pairs={{0,1},{1,2},{2,3},{3,4},{4,5},{5,6},{6,7},{7,8},{8,9},{9,10},{10,1... | collective-permute-start | bytes 2752520 | tf_op jit(solution)/shard_map/ppermute | solution.py:19
  320.9 0.8 copy-start.30
  320.9 191.1 %dynamic-slice-start = ((f32[8192]{0:T(1024)}, s32[]{:T(128)}), f32[2048]{0:T(1024)S(1)}, s32[]{:S(2)}) async-start(f32[8192]{0:T(1024)} %param.12, s32[]{:T(128)} %select_n.198), calls=%async_computation.8 | async-start | bytes 16896 | tf_op jit(solution)/shard_map/dynamic_slice | solution.py:58
  321.0 357.8 %all-reduce.8.cloned.1.call-start = ((), (), s32[]{:S(2)}) async-start(), calls=%async_computation.2 | async-start | bytes 8388608 | tf_op jit(solution)/shard_map/psum | solution.py:33
  516.4 3.4 copy-start
  522.3 226.8 %all-reduce.14.cloned.1.call-start = ((), (), s32[]{:S(2)}) async-start(), calls=%async_computation.5 | async-start | bytes 6291456 | tf_op jit(solution)/shard_map/psum | solution.py:33
  681.2 406.3 %all-reduce.10.cloned.1.call-start = ((), (), s32[]{:S(2)}) async-start(), calls=%async_computation.3 | async-start | bytes 8388608 | tf_op jit(solution)/shard_map/psum | solution.py:33
  843.9 51.9 %copy-start.14 = (f32[512,512]{1,0:T(8,128)}, f32[512,512]{1,0:T(8,128)S(1)}, u32[]{:S(2)}) copy-start(f32[512,512]{1,0:T(8,128)S(1)} %get-tuple-element.217) | copy-start | bytes 3145732
  883.2 4.8 copy-start.17
  885.1 8.2 copy-start.4
  887.3 7.4 copy-start.11
  888.0 7.8 copy-start.7
  890.5 6.4 copy-start.9
  896.8 11.2 slice-start
  897.9 10.1 copy-start.2
  901.1 6.9 slice-start.1
  902.2 3.7 copy-start.5
  925.3 3.4 copy-start.1
  931.0 226.7 %all-reduce.12.cloned.1.call-start = ((), (), s32[]{:S(2)}) async-start(), calls=%async_computation.4 | async-start | bytes 6291456 | tf_op jit(solution)/shard_map/psum | solution.py:33
  1101.5 9.4 copy-start.3
  1101.5 9.4 copy-start.6
  1254.0 49.1 %copy-start.13 = (f32[512,512]{1,0:T(8,128)}, f32[512,512]{1,0:T(8,128)S(1)}, u32[]{:S(2)}) copy-start(f32[512,512]{1,0:T(8,128)S(1)} %get-tuple-element.216) | copy-start | bytes 3145732
  1293.3 4.5 copy-start.16
  1300.4 3.4 copy-start.12
  1303.8 0.8 copy-start.18
  1323.7 5.9 copy-start.10
  1332.9 6.9 copy-start.8
  1337.3 2.5 copy-start.15
Sparse Core Ops, SparseCore 0:
  321.1 190.9 reduce-scatter.1
  522.5 156.2 all-reduce.7
  681.4 67.6 all-reduce.13
  931.1 156.3 all-reduce.9
  1090.0 67.6 all-reduce.11
